TPU v7x, 32 devices: a whole 2x2x4 slice. The times are simulated.
32 devices in a mesh: row: 4 (over x, core), col: 8 (over z, y).
Axes of the slice: x: 2, y: 2, z: 4, core: 2. Of those that a mesh axis runs over, the one named last changes fastest.
Arguments:
- covariates: float32 [16, 8192], P(None, ('row', 'col')), may hold values from -6 to 6
- lengthscale: float32 [16], replicated, may hold values from 1 to 3
- nugget: float32 [8192], P(('row', 'col')), may hold values from 0.5 to 2
- patch_values: bfloat16 [8192, 16, 128], P(('row', 'col')), may hold values from -6 to 6
- patch_weights: bfloat16 [8192, 8, 128], P(('row', 'col')), may hold values from 0 to 0.1796875
- block_index: int32 [8192, 8], P(('row', 'col')), may hold values from 0 to 255
- slot_count: int32 [8192], P(('row', 'col')), may hold values from 1 to 8
- owner: int32 [8192, 1], P(('row', 'col')), may hold values from 0 to 31; in each aligned block of 256 rows (0 to 255, 256 to 511, ...) at most 16 rows name the same one
Outputs:
- solution: float32 [16, 8192], P(None, ('row', 'col'))
- residual: float32 [16, 8192], P(None, ('row', 'col'))
Inputs may be any that keep to these rules, and one draw needn't show every extreme that they name: Among the 256 patches held by one device, no owner is named more than 16 times.
All inputs are finite; a program needn't handle non-finite values.
Results may differ from a plain program's by a relative error of at most 0.00045.
Values may be sent and summed in bfloat16 or wider, within the bound.
A program may use at most 64 MiB of HBM per device.

v0:
```python
import math

import jax
import jax.numpy as jnp
from jax import lax
from jax.sharding import PartitionSpec as P

ITERS = 2


ROOT_FIVE = 5.0**0.5
HIGH = lax.Precision.HIGHEST


def matern(left, right):
    cross = lax.dot_general(
        left, right, (((0,), (0,)), ((), ())), precision=HIGH, preferred_element_type=jnp.float32
    )
    squared = (
        jnp.sum(left * left, axis=0)[:, None]
        + jnp.sum(right * right, axis=0)[None, :]
        - 2.0 * cross
    )
    scaled = ROOT_FIVE * jnp.sqrt(jnp.maximum(squared, 0.0))
    return (1.0 + scaled + scaled * scaled / 3.0) * jnp.exp(-scaled)


def slot_table(owner, capacity, devices):
    target = owner[:, 0]
    held = target.shape[0]
    earlier = jnp.arange(held)[None, :] < jnp.arange(held)[:, None]
    rank = jnp.sum(((target[:, None] == target[None, :]) & earlier).astype(jnp.int32), axis=1)
    position = target * capacity + rank
    return position[None, :] == jnp.arange(devices * capacity)[:, None]


def both_products(residual, image):
    return lax.psum(
        (jnp.sum(residual * residual, axis=1), jnp.sum(residual * image, axis=1)), ("row", "col")
    )


def local(
    covariates, lengthscale, nugget, patch_values, patch_weights, block_index, slot_count, owner
):
    devices = lax.axis_size(("row", "col"))
    held, members, cells = patch_values.shape
    slots = patch_weights.shape[1]
    stations = nugget.shape[0]
    capacity = max(2, 2 * held // devices)
    table = slot_table(owner, capacity, devices)
    table_int = table.astype(jnp.int32)
    placed_index = jnp.dot(table_int, block_index, preferred_element_type=jnp.int32).reshape(
        devices, capacity, slots
    )
    local_terms = jnp.einsum(
        "psc,pmc->pms", patch_weights, patch_values, preferred_element_type=jnp.float32
    )
    live = (jnp.arange(slots)[None, :] < slot_count[:, None]).astype(jnp.float32)
    local_terms = (local_terms * live[:, None, :]).reshape(held, members * slots)
    placed_terms = jnp.dot(
        table.astype(jnp.float32), local_terms, precision=HIGH, preferred_element_type=jnp.float32
    )
    placed_terms = placed_terms.reshape(devices, capacity, members * slots)
    terms, index = (
        lax.all_to_all(placed_terms, ("row", "col"), split_axis=0, concat_axis=0, tiled=True),
        lax.all_to_all(placed_index, ("row", "col"), split_axis=0, concat_axis=0, tiled=True),
    )
    terms = terms.reshape(devices, capacity, members, slots)
    flat_terms = jnp.transpose(terms.reshape(-1, members, slots), (1, 0, 2)).reshape(members, -1)
    onehot = (index.reshape(-1)[:, None] == jnp.arange(stations)[None, :]).astype(jnp.float32)
    rhs = jnp.dot(flat_terms, onehot, precision=HIGH, preferred_element_type=jnp.float32)
    scaled_cov = covariates / lengthscale[:, None]
    row_cov = lax.all_gather(scaled_cov, "col", axis=1, tiled=True)

    def operate(direction):
        empty = jnp.zeros((direction.shape[0], row_cov.shape[1]), jnp.float32)
        column_cov = lax.all_gather(scaled_cov, "row", axis=1, tiled=True)
        vector = lax.all_gather(direction, "row", axis=1, tiled=True)
        width = math.gcd(vector.shape[1], 128)

        def one_block(step, acc):
            block_cov = lax.dynamic_slice_in_dim(column_cov, step * width, width, 1)
            block_vec = lax.dynamic_slice_in_dim(vector, step * width, width, 1)
            kernel = matern(block_cov, row_cov)
            return acc + jnp.dot(
                block_vec, kernel, precision=HIGH, preferred_element_type=jnp.float32
            )

        partial_value = lax.fori_loop(0, vector.shape[1] // width, one_block, empty)
        image = lax.psum_scatter(partial_value, "col", scatter_dimension=1, tiled=True)
        return image + nugget[None, :] * direction

    solution = jnp.zeros_like(rhs)
    residual = rhs
    image = operate(residual)
    norm_now, product = both_products(residual, image)
    alpha = norm_now / product
    direction = residual
    along = image
    for step in range(ITERS):
        solution = solution + alpha[:, None] * direction
        residual = residual - alpha[:, None] * along
        if step + 1 < ITERS:
            image = operate(residual)
            norm_next, product = both_products(residual, image)
            ratio = norm_next / norm_now
            alpha = norm_next / (product - ratio * norm_next / alpha)
            direction = residual + ratio[:, None] * direction
            along = image + ratio[:, None] * along
            norm_now = norm_next
    return (solution, residual)


def solution(mesh):
    placed = (
        P(None, ("row", "col")),
        P(),
        P(("row", "col")),
        P(("row", "col"), None, None),
        P(("row", "col"), None, None),
        P(("row", "col"), None),
        P(("row", "col")),
        P(("row", "col"), None),
    )
    return jax.shard_map(
        local,
        mesh=mesh,
        in_specs=placed,
        out_specs=(P(None, ("row", "col")), P(None, ("row", "col"))),
        check_vma=False,
    )
```

profile of v0, /device:TPU:0, one launch (start us, length us, event | category | flops | bytes accessed | tf_op | source)
XLA Modules:
  0.0 348.4 jit_solution(5167527160239381855)
XLA Ops:
  10.8 7.3 %all-to-all-start.1 = ((s32[32,1,128]{2,1,0:T(1,128)}), s32[32,1,128]{2,1,0:T(1,128)S(1)}, u32[]{:S(2)}, u32[]{:S(2)}) async-start(s32[32,1,128]{2,1,0:T(1,128)} %reshape.73), calls=%async_computation.1 | async-start | bytes 32768 | tf_op jit(solution)/shard_map/all_to_all | solution.py:67
  19.0 1.7 convolution_multiply_fusion.2
  22.2 3.0 all-to-all-done.1
  25.2 2.8 all-to-all-start
  28.2 5.8 %all_gather.14 = f32[16,1024]{1,0:T(8,128)} all-gather(f32[16,256]{1,0:T(8,128)S(1)} %broadcast_divide_fusion), channel_id=1, replica_groups=mesh['row'=4,'col'=8] {'row'}, dimensions={1}, use_global_device_ids=true | all-gather | bytes 81920 | tf_op jit(solution)/shard_map/all_gather | solution.py:78
  34.0 31.0 %all_gather.15 = f32[16,2048]{1,0:T(8,128)S(1)} all-gather(f32[16,256]{1,0:T(8,128)S(1)} %broadcast_divide_fusion), channel_id=1, replica_groups=mesh['row'=4,'col'=8] {'col'}, dimensions={1}, use_global_device_ids=true | all-gather | bytes 147456 | tf_op jit(solution)/shard_map/all_gather | solution.py:74
  67.8 1.8 copy.23
  72.1 3.1 fusion.38
  75.2 5.2 %all_gather.13 = f32[16,1024]{1,0:T(8,128)S(1)} all-gather(f32[16,256]{1,0:T(8,128)S(1)} %fusion.38), channel_id=1, replica_groups=mesh['row'=4,'col'=8] {'row'}, dimensions={1}, use_global_device_ids=true | all-gather | bytes 81920 | tf_op jit(solution)/shard_map/all_gather | solution.py:79
  80.4 23.7 %while.32 = (s32[]{:T(128)}, f32[16,2048]{1,0:T(8,128)S(1)}, f32[16,1024]{1,0:T(8,128)S(1)}, f32[16,1024]{1,0:T(8,128)S(1)}, f32[2048]{0:T(1024)}, /*index=5*/f3...) while((s32[]{:T(128)}, f32[16,2048]{1,0:T(8,128)S(1)}, ...), condition=%wide.region_6.0_spmd.clone, body=%wide.region_4.6_spmd.clone.sunk | while | flops 103616384 | bytes 2524329 | solution.py:90
  80.4 2.1 fusion.69
  83.4 2.1 fusion.69
  86.4 2.1 fusion.69
  89.3 2.1 fusion.69
  92.3 2.1 fusion.69
  95.3 2.1 fusion.69
  98.3 2.1 fusion.69
  101.2 2.1 fusion.69
  104.9 62.2 %reduce-scatter.3.cloned.1.call-done = f32[16,256]{1,0:T(8,128)} async-done(((f32[16,2048]{1,0:T(8,128)}), f32[16,256]{1,0:T(8,128)}) %reduce-scatter.3.cloned.1.call-update) | async-done | bytes 16400 | tf_op jit(solution)/shard_map/reduce_scatter | solution.py:91
  167.9 40.3 %all-reduce.1 = (f32[16]{0:T(128)S(1)}, f32[16]{0:T(128)S(1)}) all-reduce(f32[16]{0:T(128)S(1)} %get-tuple-element.315, f32[16]{0:T(128)S(1)} %get-tuple-element.314), channel_id=1, replica_groups=mesh['row'=4,'col'=8] {'row','col'}, use_global_device_ids=true, to_apply=%region_2.3 | all-reduce | flops 32 | bytes 256 | tf_op jit(solution)/shard_map/psum | solution.py:38
  209.0 5.5 %all_gather.16 = f32[16,1024]{1,0:T(8,128)S(1)} all-gather(f32[16,256]{1,0:T(8,128)S(1)} %multiply_subtract_fusion.1), channel_id=1, replica_groups=mesh['row'=4,'col'=8] {'row'}, dimensions={1}, use_global_device_ids=true | all-gather | bytes 81920 | tf_op jit(solution)/shard_map/all_gather | solution.py:79
  214.5 23.8 %while.33 = (s32[]{:T(128)}, f32[16,2048]{1,0:T(8,128)S(1)}, f32[16,1024]{1,0:T(8,128)S(1)}, f32[16,1024]{1,0:T(8,128)S(1)}, f32[2048]{0:T(1024)}, /*index=5*/f3...) while((s32[]{:T(128)}, f32[16,2048]{1,0:T(8,128)S(1)}, ...), condition=%wide.region_14.0_spmd.clone, body=%wide.region_12.14_spmd.clone.sunk | while | flops 103616384 | bytes 2524329 | solution.py:90
  214.5 2.1 fusion.74
  217.5 2.1 fusion.74
  220.5 2.1 fusion.74
  223.4 2.1 fusion.74
  226.4 2.1 fusion.74
  229.4 2.1 fusion.74
  232.4 2.1 fusion.74
  235.3 2.1 fusion.74
  238.9 60.2 %reduce-scatter.5.cloned.1.call-done = f32[16,256]{1,0:T(8,128)} async-done(((f32[16,2048]{1,0:T(8,128)}), f32[16,256]{1,0:T(8,128)}) %reduce-scatter.5.cloned.1.call-update) | async-done | bytes 16400 | tf_op jit(solution)/shard_map/reduce_scatter | solution.py:91
  300.0 40.1 %all-reduce = (f32[16]{0:T(128)S(1)}, f32[16]{0:T(128)S(1)}) all-reduce(f32[16]{0:T(128)S(1)} %get-tuple-element.313, f32[16]{0:T(128)S(1)} %get-tuple-element.312), channel_id=1, replica_groups=mesh['row'=4,'col'=8] {'row','col'}, use_global_device_ids=true, to_apply=%region_11.12 | all-reduce | flops 32 | bytes 256 | tf_op jit(solution)/shard_map/psum | solution.py:38
  (82 shorter events, 30.1 us)
Async XLA Ops:
  7.2 11.8 %copy-start = (bf16[256,16,128]{2,1,0:T(8,128)(2,1)S(1)}, bf16[256,16,128]{2,1,0:T(8,128)(2,1)}, u32[]{:S(2)}) copy-start(bf16[256,16,128]{2,1,0:T(8,128)(2,1)} %param.15) | copy-start | bytes 3145732
  10.8 14.3 %all-to-all-start.1 = ((s32[32,1,128]{2,1,0:T(1,128)}), s32[32,1,128]{2,1,0:T(1,128)S(1)}, u32[]{:S(2)}, u32[]{:S(2)}) async-start(s32[32,1,128]{2,1,0:T(1,128)} %reshape.73), calls=%async_computation.1 | async-start | bytes 32768 | tf_op jit(solution)/shard_map/all_to_all | solution.py:67
  19.0 9.1 %copy-start.7 = (f32[16,256]{1,0:T(8,128)S(1)}, f32[16,256]{1,0:T(8,128)}, u32[]{:S(2)}) copy-start(f32[16,256]{1,0:T(8,128)} %param.12) | copy-start | bytes 49156
  19.0 9.1 %copy-start.8 = (f32[16]{0:T(128)S(1)}, f32[16]{0:T(128)}, u32[]{:S(2)}) copy-start(f32[16]{0:T(128)} %param.13) | copy-start | bytes 196
  25.2 42.6 %all-to-all-start = ((f32[32,16,128]{2,1,0:T(8,128)}), f32[32,16,128]{2,1,0:T(8,128)S(1)}, u32[]{:S(2)}, u32[]{:S(2)}) async-start(f32[32,16,128]{2,1,0:T(8,128)} %fusion.41), calls=%async_computation | async-start | bytes 524288 | tf_op jit(solution)/shard_map/all_to_all | solution.py:66
  28.0 139.0 %reduce-scatter.3.cloned.1.call-start = ((), (), s32[]{:S(2)}) async-start(), calls=%async_computation.4 | async-start | bytes 147456 | tf_op jit(solution)/shard_map/reduce_scatter | solution.py:91
  72.1 8.3 %copy-start.1 = (f32[16,1024]{1,0:T(8,128)S(1)}, f32[16,1024]{1,0:T(8,128)}, u32[]{:S(2)}) copy-start(f32[16,1024]{1,0:T(8,128)} %all_gather.14) | copy-start | bytes 196612
  72.1 8.3 %copy-start.3 = (f32[16,2048]{1,0:T(8,128)S(1)}, f32[16,2048]{1,0:T(8,128)}, u32[]{:S(2)}) copy-start(f32[16,2048]{1,0:T(8,128)} %custom-call) | copy-start | bytes 393220
  80.4 86.7 %copy-start.6 = (f32[256]{0:T(256)S(1)}, f32[256]{0:T(256)}, u32[]{:S(2)}) copy-start(f32[256]{0:T(256)} %param.14) | copy-start | bytes 3076
  104.2 0.6 copy-start.4
  104.8 194.3 %reduce-scatter.5.cloned.1.call-start = ((), (), s32[]{:S(2)}) async-start(), calls=%async_computation.5 | async-start | bytes 147456 | tf_op jit(solution)/shard_map/reduce_scatter | solution.py:91
  214.5 125.6 %copy-start.2 = (f32[16,256]{1,0:T(8,128)S(1)}, f32[16,256]{1,0:T(8,128)}, u32[]{:S(2)}) copy-start(f32[16,256]{1,0:T(8,128)} %reduce-scatter.3.cloned.1.call-done) | copy-start | bytes 49156
  238.3 0.6 copy-start.5
Sparse Core Ops, SparseCore 0:
  104.9 62.0 reduce-scatter.2
  239.1 60.0 reduce-scatter.4
where the time goes:
time: 350 us; the launch traced here: 348 us
  blocking collectives  128 us (37%)
  waiting for transfers between devices  125 us (36%)
  matrix products  53.5 us (15%)
  between operations  14.3 us (4%)
  starting transfers between devices  10.2 us (3%)
  local copies, waits for them, and re-layouts  8.28 us (2%)
  other arithmetic  8.09 us (2%)
    reduce_scatter x2, waiting for transfers between devices, operate(): lax.psum_scatter(partial_value, 'col', scatter_dimension=1, tiled=True)  122 us
    psum x2, blocking collectives, both_products(): lax.psum((jnp.sum(residual * residual, axis=1), jnp.sum(residual * image,...  80.4 us
    dot_general x16, matrix products, matern(): lax.dot_general(left, right, (((0,), (0,)), ((), ())), precision=HIGH, pr...  33.3 us
    all_gather x1, blocking collectives, local(): row_cov = lax.all_gather(scaled_cov, 'col', axis=1, tiled=True)  31 us
    dot_general x16, matrix products, one_block(): jnp.dot(block_vec, kernel, precision=HIGH, preferred_element_type=jnp.flo...  13.2 us
    all_gather x2, blocking collectives, operate(): vector = lax.all_gather(direction, 'row', axis=1, tiled=True)  10.8 us
    all_to_all x1, starting transfers between devices, local(): lax.all_to_all(placed_index, ('row', 'col'), split_axis=0, concat_axis=0,...  7.3 us
  transfers between devices with their start and end apart: 4, of which 3 were waited for; matrix products, arithmetic and copies ran while one was open for 2% of the time, Pallas kernels for 0%

commit v1 on v0

v1 whole, which is shorter than its diff:
```python
import functools
import math

import jax
import jax.numpy as jnp
from jax import lax
from jax.experimental import pallas as pl
from jax.experimental.pallas import tpu as pltpu
from jax.sharding import PartitionSpec as P

MESH = pl.DeviceIdType.MESH
F32, BF16 = jnp.float32, jnp.bfloat16
LOG2E = 1.0 / math.log(2.0)
SCALE = 5.0 * LOG2E * LOG2E
LINEAR = math.log(2.0)
SQUARE = math.log(2.0) ** 2 / 3.0


def iota(shape, axis):
    return lax.broadcasted_iota(jnp.int32, shape, axis)


def mm(a, b):
    return jnp.dot(a, b, preferred_element_type=F32)


def mm_nt(a, b):
    return lax.dot_general(a, b, (((1,), (1,)), ((), ())), preferred_element_type=F32)


def split2(x):
    hi = x.astype(BF16)
    return hi, (x - hi.astype(F32)).astype(BF16)


def split3(x):
    hi = x.astype(BF16).astype(F32)
    rest = x - hi
    mid = rest.astype(BF16).astype(F32)
    return hi, mid, rest - mid


def stack(parts, rows):
    place = iota((rows, parts[0].shape[1]), 0)
    out = jnp.zeros((rows, parts[0].shape[1]), F32)
    for number, part in enumerate(parts):
        out = jnp.where(place == number, part, out)
    return out


def features(z, left):
    feats, width = z.shape
    norm = split3(SCALE * jnp.sum(z * z, axis=0, keepdims=True))
    ones = [jnp.ones((1, width), F32)] * 3
    hi, mid, low = split3(z * (-2.0 * SCALE)) if left else split3(z)
    if left:
        parts, tail = [hi, hi, mid, mid, hi, low], list(norm) + ones
    else:
        parts, tail = [hi, mid, hi, mid, low, hi], ones + list(norm)
    used = 6 * feats + 8
    padded = -(-used // 128) * 128
    parts = parts + [stack(tail, 8)]
    if padded > used:
        parts.append(jnp.zeros((padded - used, width), F32))
    return jnp.concatenate(parts, axis=0)


def kernel(
    rows, cols, cap,
    cov, ls, nug, val, wts, idx, cnt, own,
    sol, res,
    zrow, zcol, left, right, k_hi, k_lo,
    tsend, trecv, isend, irecv, vrow, vcol, pout, pin, scal,
    zr_s, zr_r, zc_s, zc_r, t_s, t_r, i_s, i_r,
    vr_s, vr_r, vc_s, vc_r, p_s, p_r, s_s, s_r,
):
    devices = rows * cols
    r, c = lax.axis_index("row"), lax.axis_index("col")
    me = r * cols + c
    feats, st = cov.shape
    held, slots = idx.shape
    members = val.shape[0] // held
    group = 128 // slots

    def place(k):
        other = lax.rem(me + k, devices)
        return other, (lax.div(other, cols), lax.rem(other, cols))

    barrier = pltpu.get_barrier_semaphore()

    def greet(k, carry):
        pl.semaphore_signal(barrier, inc=1, device_id=place(k)[1], device_id_type=MESH)
        return carry

    lax.fori_loop(1, devices, greet, 0)

    def row_copy(buf, ss, rs, k, slot):
        other = lax.rem(r + k, rows)
        at = r if slot is None else other
        return pltpu.make_async_remote_copy(
            src_ref=buf.at[at], dst_ref=buf.at[at], send_sem=ss.at[other], recv_sem=rs.at[at],
            device_id=(other, c), device_id_type=MESH)

    def col_copy(src, buf, ss, rs, k, slot):
        other = lax.rem(c + k, cols)
        at = c if slot is None else other
        return pltpu.make_async_remote_copy(
            src_ref=src.at[other] if src is not buf else buf.at[at], dst_ref=buf.at[at],
            send_sem=ss.at[other], recv_sem=rs.at[at],
            device_id=(r, other), device_id_type=MESH)

    def all_copy(src, buf, ss, rs, k, slot):
        other, where = place(k)
        at = me if slot is None else other
        return pltpu.make_async_remote_copy(
            src_ref=src.at[other] if src is not buf else buf.at[at], dst_ref=buf.at[at],
            send_sem=ss.at[other], recv_sem=rs.at[at],
            device_id=where, device_id_type=MESH)

    def each(count, act):
        def step(k, carry):
            act(k)
            return carry
        lax.fori_loop(1, count, step, 0)

    diag = iota((feats, feats), 0) == iota((feats, feats), 1)
    scale = jnp.sum(jnp.where(diag, ls[...], 0.0), axis=1, keepdims=True)
    z = cov[...] / scale
    zrow[r] = z
    zcol[c] = z

    eye = iota((held, held), 0) == iota((held, held), 1)
    own_col = own[...].astype(F32)
    own_row = jnp.sum(jnp.where(eye, own_col, 0.0), axis=0, keepdims=True)
    cnt_col = jnp.sum(jnp.where(eye, cnt[...].astype(F32), 0.0), axis=1, keepdims=True)
    same = (own_col == own_row) & (iota((held, held), 1) < iota((held, held), 0))
    rank = jnp.sum(jnp.where(same, 1.0, 0.0), axis=1, keepdims=True)
    position = own_col * cap + rank

    live = iota((held, slots), 1).astype(F32) < cnt_col
    station = jnp.where(live, idx[...].astype(F32), float(st))
    spread = jnp.where(iota((slots, 128), 1) % slots == iota((slots, 128), 0), 1.0, 0.0)
    wide = mm(station.astype(BF16), spread.astype(BF16))
    wide = jnp.where((iota((held, 128), 1) // slots).astype(F32) == rank, wide, 0.0)
    to_owner = jnp.where(iota((devices, held), 0).astype(F32) == own_row, 1.0, 0.0)
    index_rows = mm(to_owner.astype(BF16), wide.astype(BF16))
    for o in range(devices):
        isend[o] = index_rows[o : o + 1]

    blocks = iota((group, members, 128), 0) == iota((group, members, 128), 2) // slots
    lane_patch = iota((group, 128), 1) // slots == iota((group, 128), 0)
    slot_of = iota((members, 128), 1) % slots
    total = jnp.zeros((devices * cap, 2 * slots * members), F32)
    tables, spreads = [], []
    for g in range(held // group):
        cross = mm_nt(
            val[g * group * members : (g + 1) * group * members, :],
            wts[g * 128 : (g + 1) * 128, :],
        ).reshape(group, members, 128)
        terms = jnp.sum(jnp.where(blocks, cross, 0.0), axis=0)
        hi = terms.astype(BF16).astype(F32)
        low = terms - hi
        by_slot = [jnp.where(slot_of == s, part, 0.0) for part in (hi, low) for s in range(slots)]
        spreads.append(jnp.concatenate(by_slot, axis=0).astype(BF16))
        at = jnp.sum(
            jnp.where(lane_patch, position[g * group : (g + 1) * group], 0.0), axis=0, keepdims=True)
        tables.append(
            jnp.where(iota((devices * cap, 128), 0).astype(F32) == at, 1.0, 0.0).astype(BF16))
        if len(tables) == 4 or g + 1 == held // group:
            total = total + mm_nt(jnp.concatenate(tables, axis=1), jnp.concatenate(spreads, axis=1))
            tables, spreads = [], []
    packed = total[:, : slots * members] + total[:, slots * members :]
    tsend[...] = packed.reshape(devices, cap, slots * members)
    trecv[me] = tsend[me]
    irecv[me] = isend[me]

    pl.semaphore_wait(barrier, devices - 1)
    each(rows, lambda k: row_copy(zrow, zr_s, zr_r, k, None).start())
    each(cols, lambda k: col_copy(zcol, zcol, zc_s, zc_r, k, None).start())

    def send_terms(k):
        all_copy(tsend, trecv, t_s, t_r, k, None).start()
        all_copy(isend, irecv, i_s, i_r, k, None).start()

    each(devices, send_terms)

    each(rows, lambda k: row_copy(zrow, zr_s, zr_r, k, 1).wait_recv())
    for i in range(rows):
        left[i * st : (i + 1) * st, :] = features(zrow[i], True).T.astype(BF16)
    each(cols, lambda k: col_copy(zcol, zcol, zc_s, zc_r, k, 1).wait_recv())

    def make_right(i, carry):
        right[i] = features(zcol[i], False).astype(BF16)
        return carry

    lax.fori_loop(0, cols, make_right, 0)

    chunk = 128
    chunks = rows * st // chunk

    def make_kernel(t, carry):
        j, i = lax.div(t, chunks), lax.rem(t, chunks)
        here = pl.ds(pl.multiple_of(i * chunk, chunk), chunk)
        square = jnp.maximum(mm(left[here, :], right[j]), 1e-30)
        w = square * lax.rsqrt(square)
        value = (1.0 + LINEAR * w + SQUARE * square) * jnp.exp2(-w)
        hi, low = split2(value)
        k_hi[j, here, :] = hi
        k_lo[j, here, :] = low
        return carry

    lax.fori_loop(0, cols * chunks, make_kernel, 0)

    def wait_terms(k):
        all_copy(tsend, trecv, t_s, t_r, k, 1).wait_recv()
        all_copy(isend, irecv, i_s, i_r, k, 1).wait_recv()

    each(devices, wait_terms)
    got = devices * cap
    rep = jnp.where(iota((got, devices), 0) // cap == iota((got, devices), 1), 1.0, 0.0)
    seen = irecv[...].reshape(devices, 128)
    z_rows = mm(rep.astype(BF16), seen.astype(BF16))
    z_rows = jnp.where(iota((got, 128), 0) % cap == iota((got, 128), 1) // slots, z_rows, 0.0)
    by_slot = mm_nt(spread.astype(BF16), z_rows.astype(BF16))
    flat = trecv[...].reshape(got, slots * members).T
    names = iota((st, got), 0).astype(F32)
    rhs2 = jnp.zeros((2 * members, st), F32)
    for s in range(slots):
        hi, low = split2(flat[s * members : (s + 1) * members])
        hit = jnp.where(names == by_slot[s : s + 1], 1.0, 0.0).astype(BF16)
        rhs2 = rhs2 + mm_nt(jnp.concatenate([hi, low], axis=0), hit)
    rhs = rhs2[:members] + rhs2[members:]

    lane, sub = iota((members, 128), 1), iota((members, 128), 0)

    def operate(turn, v):
        vr, vc = vrow.at[turn], vcol.at[turn]
        vr[r] = v
        vc[c] = v
        each(rows, lambda k: row_copy(vr, vr_s.at[turn], vr_r.at[turn], k, None).start())
        each(cols, lambda k: col_copy(vc, vc, vc_s.at[turn], vc_r.at[turn], k, None).start())
        each(rows, lambda k: row_copy(vr, vr_s.at[turn], vr_r.at[turn], k, 1).wait_recv())
        whole = jnp.concatenate([vr[i] for i in range(rows)], axis=1)
        hi, low = split2(whole)
        both = jnp.concatenate([hi, low], axis=0)
        each(cols, lambda k: col_copy(vc, vc, vc_s.at[turn], vc_r.at[turn], k, 1).wait_recv())

        def part(other):
            double = mm(both, k_hi[other])
            return double[:members] + double[members:] + mm(hi, k_lo[other])

        def one(k, acc):
            other = lax.rem(c + k, cols)
            mine = part(other)
            pout[turn, other] = mine
            col_copy(pout.at[turn], pin.at[turn], p_s.at[turn], p_r.at[turn], k, None).start()
            return acc + mine * vc[other]

        acc = lax.fori_loop(1, cols, one, jnp.zeros((members, st), F32))
        mine = part(c)
        pin[turn, c] = mine
        shift = nug[...] * v
        acc = acc + (mine + shift) * v
        norm = jnp.sum(v * v, axis=1, keepdims=True)
        product = jnp.sum(acc, axis=1, keepdims=True)
        line = jnp.where(lane == sub, norm, 0.0) + jnp.where(lane == sub + members, product, 0.0)
        sc = scal.at[turn]
        sc[me] = jnp.sum(line, axis=0, keepdims=True)
        each(devices, lambda k: all_copy(sc, sc, s_s.at[turn], s_r.at[turn], k, None).start())
        each(cols, lambda k: col_copy(
            pout.at[turn], pin.at[turn], p_s.at[turn], p_r.at[turn], k, 1).wait_recv())
        image = shift + jnp.sum(pin[turn], axis=0)
        each(devices, lambda k: all_copy(sc, sc, s_s.at[turn], s_r.at[turn], k, 1).wait_recv())
        sums = jnp.sum(sc[...], axis=0)
        norm = jnp.sum(jnp.where(lane == sub, sums, 0.0), axis=1, keepdims=True)
        product = jnp.sum(jnp.where(lane == sub + members, sums, 0.0), axis=1, keepdims=True)
        return image, norm, product

    image, norm, product = operate(0, rhs)
    alpha = norm / product
    residual = rhs - alpha * image
    image_next, norm_next, product = operate(1, residual)
    ratio = norm_next / norm
    alpha_next = norm_next / (product - ratio * norm_next / alpha)
    sol[...] = alpha * rhs + alpha_next * (residual + ratio * rhs)
    res[...] = residual - alpha_next * (image_next + ratio * image)

    each(rows, lambda k: row_copy(zrow, zr_s, zr_r, k, 1).wait_send())
    each(cols, lambda k: col_copy(zcol, zcol, zc_s, zc_r, k, 1).wait_send())

    def sent(k):
        all_copy(tsend, trecv, t_s, t_r, k, 1).wait_send()
        all_copy(isend, irecv, i_s, i_r, k, 1).wait_send()
        for turn in range(2):
            sc = scal.at[turn]
            all_copy(sc, sc, s_s.at[turn], s_r.at[turn], k, 1).wait_send()

    each(devices, sent)
    for turn in range(2):
        vr, vc = vrow.at[turn], vcol.at[turn]
        each(rows, lambda k: row_copy(vr, vr_s.at[turn], vr_r.at[turn], k, 1).wait_send())
        each(cols, lambda k: col_copy(vc, vc, vc_s.at[turn], vc_r.at[turn], k, 1).wait_send())
        each(cols, lambda k: col_copy(
            pout.at[turn], pin.at[turn], p_s.at[turn], p_r.at[turn], k, 1).wait_send())


def local(rows, cols, covariates, lengthscale, nugget, patch_values, patch_weights, block_index,
          slot_count, owner):
    devices = rows * cols
    feats, st = covariates.shape
    held, members, cells = patch_values.shape
    slots = patch_weights.shape[1]
    cap = max(128 // slots, 2 * held // devices)
    wide = -(-(6 * feats + 8) // 128) * 128
    dma = pltpu.SemaphoreType.DMA
    vmem = pltpu.VMEM
    scratch = [
        vmem((rows, feats, st), F32),
        vmem((cols, feats, st), F32),
        vmem((rows * st, wide), BF16),
        vmem((cols, wide, st), BF16),
        vmem((cols, rows * st, st), BF16),
        vmem((cols, rows * st, st), BF16),
        vmem((devices, cap, slots * members), F32),
        vmem((devices, cap, slots * members), F32),
        vmem((devices, 1, 128), F32),
        vmem((devices, 1, 128), F32),
        vmem((2, rows, members, st), F32),
        vmem((2, cols, members, st), F32),
        vmem((2, cols, members, st), F32),
        vmem((2, cols, members, st), F32),
        vmem((2, devices, 1, 128), F32),
    ]
    sems = [(rows,)] * 2 + [(cols,)] * 2 + [(devices,)] * 4
    sems += [(2, rows)] * 2 + [(2, cols)] * 4 + [(2, devices)] * 2
    scratch += [dma(shape) for shape in sems]
    spec = pl.BlockSpec(memory_space=pltpu.VMEM)
    return pl.pallas_call(
        functools.partial(kernel, rows, cols, cap),
        out_shape=[jax.ShapeDtypeStruct((members, st), F32)] * 2,
        in_specs=[spec] * 8,
        out_specs=[spec] * 2,
        scratch_shapes=scratch,
        compiler_params=pltpu.CompilerParams(
            collective_id=0, has_side_effects=True, vmem_limit_bytes=56 * 2**20),
    )(
        covariates,
        lengthscale.reshape(1, feats),
        nugget.reshape(1, st),
        patch_values.reshape(held * members, cells),
        patch_weights.reshape(held * slots, cells),
        block_index,
        slot_count.reshape(1, held),
        owner,
    )


def solution(mesh):
    placed = (
        P(None, ("row", "col")),
        P(),
        P(("row", "col")),
        P(("row", "col"), None, None),
        P(("row", "col"), None, None),
        P(("row", "col"), None),
        P(("row", "col")),
        P(("row", "col"), None),
    )
    return jax.shard_map(
        functools.partial(local, mesh.shape["row"], mesh.shape["col"]),
        mesh=mesh,
        in_specs=placed,
        out_specs=(P(None, ("row", "col")), P(None, ("row", "col"))),
        check_vma=False,
    )
```

time: 350 us -> 61.9 us (0.18)
  blocking collectives: 128 us -> 0 us
  waiting for transfers between devices: 125 us -> 0 us
  Pallas kernels: 0 us -> 56.8 us
  matrix products: 53.5 us -> 0 us
  between operations: 14.3 us -> 0.66 us
  starting transfers between devices: 10.2 us -> 0 us
  other arithmetic: 8.09 us -> 0 us
  local copies, waits for them, and re-layouts: 8.28 us -> 4.19 us
    reduce_scatter x2 -> x0, waiting for transfers between devices: 122 us -> none  [operate(): lax.psum_scatter(partial_value, 'col', scatter_dimension=1, tiled=True)]
    psum x2 -> x0, blocking collectives: 80.4 us -> none  [both_products(): lax.psum((jnp.sum(residual * residual, axis=1), jnp.sum(residual * image,...]
    pallas_call x0 -> x1, Pallas kernels: none -> 56.8 us  [local(): pl.pallas_call(functools.partial(kernel, rows, cols, cap), out_shape=[jax...]
    dot_general x36 -> x0, matrix products: 53.5 us -> none  [the longest x16 33.3 us: matern(): lax.dot_general(left, right, (((0,), (0,)), ((), ())), precision=HIGH, pr...]
    all_gather x4 -> x0, blocking collectives: 47.6 us -> none  [the longest x1 31 us: local(): row_cov = lax.all_gather(scaled_cov, 'col', axis=1, tiled=True)]
    all_to_all x2 -> x0, starting transfers between devices: 10.1 us -> none  [the longest x1 7.3 us: local(): lax.all_to_all(placed_index, ('row', 'col'), split_axis=0, concat_axis=0,...]
    reduce_sum x20 -> x0, other arithmetic: 3.64 us -> none  [the longest x2 1.67 us: both_products(): jnp.sum(residual * image, axis=1)]
  transfers between devices with their start and end apart: 4 -> 0, of which waited for: 3 -> 0; matrix products, arithmetic and copies ran while one was open for 2% -> 0% of each run, Pallas kernels for 0% -> 0%
where the time goes in v1:
time: 61.9 us; the launch traced here: 61.7 us
  Pallas kernels  56.8 us (92%)
  local copies, waits for them, and re-layouts  4.19 us (7%)
  between operations  0.66 us (1%)
    pallas_call x1, Pallas kernels, local(): pl.pallas_call(functools.partial(kernel, rows, cols, cap), out_shape=[jax...  56.8 us
    unnamed x10, local copies, waits for them, and re-layouts  4.19 us

profile of v1, /device:TPU:0, one launch (start us, length us, event | category | flops | bytes accessed | tf_op | source)
XLA Modules:
  0.0 61.7 jit_solution(16572909343737181308)
XLA Ops:
  0.6 0.0 copy-start.1
  0.6 0.7 %copy-done.1 = s32[256,8]{0,1:T(8,128)S(1)} copy-done((s32[256,8]{0,1:T(8,128)S(1)}, s32[256,8]{0,1:T(8,128)}, u32[]{:S(2)}) %copy-start.1) | copy-done | bytes 8216
  1.3 0.0 copy-start.2
  1.3 0.8 %copy.10.idx = s32[256,8]{1,0:T(8,128)} copy(s32[256,8]{0,1:T(8,128)S(1)} %copy-done.1) | data formatting | bytes 16384 | tf_op args[5]
  2.1 0.0 copy-done.2
  2.1 0.8 %copy.11.own = s32[256,1]{1,0:T(8,128)} copy(s32[256,1]{0,1:T(1,128)S(1)} %copy-done.2) | data formatting | bytes 2048 | tf_op args[7]
  2.9 56.8 %shard_map.95 = (f32[16,256]{1,0:T(8,128)}, f32[16,256]{1,0:T(8,128)}) custom-call(f32[16,256]{1,0:T(8,128)} %cov.1, f32[1,16]{1,0:T(1,128)} %bitcast.9, f32[1,256]{1,0:T(1,128)} %bitcast.7, bf16[4096,128]{1,0:T(8,128)(2,1)} %bitcast.5, bf16[2048,128]{1,0:T(8,128)(2,1)} %bitcast.6, s32[256,8]{1,0:T(8,128)} %copy.10.idx, s32[1,256]{1,0:T(1,128)} %bitcast.8, ...), custom_call_target="tpu_custom_call" | custom-call | tf_op jit(solution)/shard_map/pallas_call | solution.py:338
  59.7 0.0 copy-start
  59.8 1.3 %copy.14 = f32[16,256]{1,0:T(8,128)} copy(f32[16,256]{1,0:T(8,128)} %get-tuple-element.4) | data formatting | bytes 32768
  61.1 0.0 copy-done
  61.1 0.6 copy.15
Async XLA Ops:
  0.6 0.7 %copy-start.1 = (s32[256,8]{0,1:T(8,128)S(1)}, s32[256,8]{0,1:T(8,128)}, u32[]{:S(2)}) copy-start(s32[256,8]{0,1:T(8,128)} %param.13) | copy-start | bytes 24580
  1.3 0.8 %copy-start.2 = (s32[256,1]{0,1:T(1,128)S(1)}, s32[256,1]{0,1:T(1,128)}, u32[]{:S(2)}) copy-start(s32[256,1]{0,1:T(1,128)} %param.15) | copy-start | bytes 3076
  59.7 1.3 %copy-start = (f32[16,256]{1,0:T(8,128)S(1)}, f32[16,256]{1,0:T(8,128)}, u32[]{:S(2)}) copy-start(f32[16,256]{1,0:T(8,128)} %get-tuple-element.5) | copy-start | bytes 49156

commit v2 on v1

v2 whole, which is shorter than its diff:
```python
import functools
import math

import jax
import jax.numpy as jnp
from jax import lax
from jax.experimental import pallas as pl
from jax.experimental.pallas import tpu as pltpu
from jax.sharding import PartitionSpec as P

MESH = pl.DeviceIdType.MESH
F32, BF16 = jnp.float32, jnp.bfloat16
LOG2E = 1.0 / math.log(2.0)
SCALE = 5.0 * LOG2E * LOG2E
LINEAR = math.log(2.0)
SQUARE = math.log(2.0) ** 2 / 3.0


def iota(shape, axis):
    return lax.broadcasted_iota(jnp.int32, shape, axis)


def mm(a, b):
    return jnp.dot(a, b, preferred_element_type=F32)


def mm_nt(a, b):
    return lax.dot_general(a, b, (((1,), (1,)), ((), ())), preferred_element_type=F32)


def split2(x):
    hi = x.astype(BF16)
    return hi, (x - hi.astype(F32)).astype(BF16)


def split3(x):
    hi = x.astype(BF16).astype(F32)
    rest = x - hi
    mid = rest.astype(BF16).astype(F32)
    return hi, mid, rest - mid


def stack(parts, rows):
    place = iota((rows, parts[0].shape[1]), 0)
    out = jnp.zeros((rows, parts[0].shape[1]), F32)
    for number, part in enumerate(parts):
        out = jnp.where(place == number, part, out)
    return out


def features(z, left):
    feats, width = z.shape
    norm = split3(SCALE * jnp.sum(z * z, axis=0, keepdims=True))
    ones = [jnp.ones((1, width), F32)] * 3
    hi, mid, low = split3(z * (-2.0 * SCALE)) if left else split3(z)
    if left:
        parts, tail = [hi, hi, mid, mid, hi, low], list(norm) + ones
    else:
        parts, tail = [hi, mid, hi, mid, low, hi], ones + list(norm)
    used = 6 * feats + 8
    padded = -(-used // 128) * 128
    parts = parts + [stack(tail, 8)]
    if padded > used:
        parts.append(jnp.zeros((padded - used, width), F32))
    return jnp.concatenate(parts, axis=0)


def kernel(
    rows, cols, cap,
    cov, ls, nug, val_hbm, wts_hbm, idx, cnt, own,
    out,
    val, wts, zrow, zcol, left, right, k_hi, k_lo,
    tsend, trecv, isend, irecv, vrow, vcol, base, pout, pin, scal,
    load, zr_s, zr_r, zc_s, zc_r, t_s, t_r, i_s, i_r,
    vr_s, vr_r, vc_s, vc_r, p_s, p_r, s_s, s_r,
):
    devices = rows * cols
    r, c = lax.axis_index("row"), lax.axis_index("col")
    me = r * cols + c
    feats, st = cov.shape
    slots, held = idx.shape
    members = val.shape[0] // held
    group = 128 // slots

    def row_of(k):
        return jnp.where(r + k >= rows, r + k - rows, r + k)

    def col_of(k):
        return jnp.where(c + k >= cols, c + k - cols, c + k)

    around = [col_of(k) for k in range(cols)]

    def to_all(act):
        for k in range(1, cols):
            act(r * cols + around[k], (r, around[k]))

        def step(k, carry):
            other = row_of(k)
            for column in around:
                act(other * cols + column, (other, column))
            return carry

        lax.fori_loop(1, rows, step, 0)

    def to_row(act):
        for k in range(1, rows):
            act(row_of(k), (row_of(k), c))

    def to_col(act):
        for k in range(1, cols):
            act(around[k], (r, around[k]))

    def push(src, dst, ss, rs, where):
        pltpu.make_async_remote_copy(
            src_ref=src, dst_ref=dst, send_sem=ss, recv_sem=rs,
            device_id=where, device_id_type=MESH).start()

    def await_all(buf, sem):
        part = buf.at[pl.ds(0, buf.shape[0] - 1)]
        pltpu.make_async_copy(part, part, sem).wait()

    loads = [pltpu.make_async_copy(val_hbm, val, load.at[0]),
             pltpu.make_async_copy(wts_hbm, wts, load.at[1])]
    for copy in loads:
        copy.start()

    barrier = pltpu.get_barrier_semaphore()
    to_all(lambda other, where: pl.semaphore_signal(
        barrier, inc=1, device_id=where, device_id_type=MESH))

    diag = iota((feats, feats), 0) == iota((feats, feats), 1)
    scale = jnp.sum(jnp.where(diag, ls[...], 0.0), axis=1, keepdims=True)
    z = cov[...] / scale
    zrow[r] = z
    zcol[c] = z

    eye = iota((held, held), 0) == iota((held, held), 1)
    own_row = own[...].astype(F32)
    own_col = jnp.sum(jnp.where(eye, own_row, 0.0), axis=1, keepdims=True)
    same = (own_col == own_row) & (iota((held, held), 1) < iota((held, held), 0))
    rank = jnp.sum(jnp.where(same, 1.0, 0.0), axis=1, keepdims=True)
    position = own_col * cap + rank

    live = iota((slots, held), 0) < cnt[...]
    station = jnp.where(live, idx[...].astype(F32), float(st))
    station = jnp.concatenate([station, jnp.zeros((128 - slots, held), F32)], axis=0).T
    spread = jnp.where(iota((128, 128), 1) % slots == iota((128, 128), 0), 1.0, 0.0)
    wide = mm(station.astype(BF16), spread.astype(BF16))
    wide = jnp.where((iota((held, 128), 1) // slots).astype(F32) == rank, wide, 0.0)
    to_owner = jnp.where(iota((devices, held), 0).astype(F32) == own_row, 1.0, 0.0)
    index_rows = mm(to_owner.astype(BF16), wide.astype(BF16))
    for o in range(devices):
        isend[o] = index_rows[o : o + 1]
    irecv[me] = isend[me]

    pl.semaphore_wait(barrier, devices - 1)
    to_row(lambda other, where: push(zrow.at[r], zrow.at[r], zr_s, zr_r, where))
    to_col(lambda other, where: push(zcol.at[c], zcol.at[c], zc_s, zc_r, where))

    for copy in loads:
        copy.wait()
    blocks = iota((group, members, 128), 0) == iota((group, members, 128), 2) // slots
    lane_patch = iota((group, 128), 1) // slots == iota((group, 128), 0)
    slot_of = iota((members, 128), 1) % slots
    total = jnp.zeros((devices * cap, 2 * slots * members), F32)
    tables, spreads = [], []
    for g in range(held // group):
        cross = mm_nt(
            val[g * group * members : (g + 1) * group * members, :],
            wts[g * 128 : (g + 1) * 128, :],
        ).reshape(group, members, 128)
        terms = jnp.sum(jnp.where(blocks, cross, 0.0), axis=0)
        hi = terms.astype(BF16).astype(F32)
        low = terms - hi
        by_slot = [jnp.where(slot_of == s, part, 0.0) for part in (hi, low) for s in range(slots)]
        spreads.append(jnp.concatenate(by_slot, axis=0).astype(BF16))
        at = jnp.sum(
            jnp.where(lane_patch, position[g * group : (g + 1) * group], 0.0), axis=0, keepdims=True)
        tables.append(
            jnp.where(iota((devices * cap, 128), 0).astype(F32) == at, 1.0, 0.0).astype(BF16))
        if len(tables) == 4 or g + 1 == held // group:
            total = total + mm_nt(jnp.concatenate(tables, axis=1), jnp.concatenate(spreads, axis=1))
            tables, spreads = [], []
    packed = total[:, : slots * members] + total[:, slots * members :]
    tsend[...] = packed.reshape(devices, cap, slots * members)
    trecv[me] = tsend[me]

    def send_terms(other, where):
        push(tsend.at[other], trecv.at[me], t_s, t_r, where)
        push(isend.at[other], irecv.at[me], i_s, i_r, where)

    to_all(send_terms)

    await_all(zrow, zr_r)
    for k in range(rows):
        left[k * st : (k + 1) * st, :] = features(zrow[row_of(k)], True).T.astype(BF16)
    await_all(zcol, zc_r)

    def make_right(k, carry):
        right[k] = features(zcol[col_of(k)], False).astype(BF16)
        return carry

    lax.fori_loop(0, cols, make_right, 0)

    chunk = 2 * st
    chunks = rows * st // chunk

    def make_kernel(j, carry):
        for i in range(chunks):
            here = pl.ds(i * chunk, chunk)
            square = jnp.maximum(mm(left[here, :], right[j]), 1e-30)
            w = square * lax.rsqrt(square)
            value = (1.0 + LINEAR * w + SQUARE * square) * jnp.exp2(-w)
            hi, low = split2(value)
            k_hi[j, here, :] = hi
            k_lo[j, here, :] = low
        return carry

    lax.fori_loop(0, cols, make_kernel, 0)

    await_all(irecv, i_r)
    got = devices * cap
    rep = jnp.where(iota((got, devices), 0) // cap == iota((got, devices), 1), 1.0, 0.0)
    seen = irecv[...].reshape(devices, 128)
    z_rows = mm(rep.astype(BF16), seen.astype(BF16))
    z_rows = jnp.where(iota((got, 128), 0) % cap == iota((got, 128), 1) // slots, z_rows, 0.0)
    by_slot = mm_nt(spread[:slots].astype(BF16), z_rows.astype(BF16))
    names = iota((st, got), 0).astype(F32)
    await_all(trecv, t_r)
    flat = trecv[...].reshape(got, slots * members).T
    rhs2 = jnp.zeros((2 * members, st), F32)
    for s in range(slots):
        hi, low = split2(flat[s * members : (s + 1) * members])
        hit = jnp.where(names == by_slot[s : s + 1], 1.0, 0.0).astype(BF16)
        rhs2 = rhs2 + mm_nt(jnp.concatenate([hi, low], axis=0), hit)
    rhs = rhs2[:members] + rhs2[members:]

    lane, sub = iota((members, 128), 1), iota((members, 128), 0)

    def operate(turn, v):
        vr, vc, sc = vrow.at[turn], vcol.at[turn], scal.at[turn]
        po, pi = pout.at[turn], pin.at[turn]
        vr[r] = v
        vc[c] = v
        to_row(lambda other, where: push(
            vr.at[r], vr.at[r], vr_s.at[turn], vr_r.at[turn], where))
        to_col(lambda other, where: push(
            vc.at[c], vc.at[c], vc_s.at[turn], vc_r.at[turn], where))

        def part(parts, k, here):
            hi, low = parts
            double = mm(jnp.concatenate([hi, low], axis=0), k_hi[k, here, :])
            return double[:members] + double[members:] + mm(hi, k_lo[k, here, :])

        mine = split2(v)
        for k in range(cols):
            base[k] = part(mine, k, pl.ds(0, st))
        await_all(vr, vr_r.at[turn])
        others = split2(jnp.concatenate([vr[row_of(k)] for k in range(1, rows)], axis=1))
        rest = pl.ds(st, (rows - 1) * st)
        for k in range(1, cols):
            total = base[k] + part(others, k, rest)
            base[k] = total
            po[around[k]] = total
            push(po.at[around[k]], pi.at[c], p_s.at[turn], p_r.at[turn], (r, around[k]))
        total = base[0] + part(others, 0, rest)
        pi[c] = total
        shift = nug[...] * v
        await_all(vc, vc_r.at[turn])
        acc = (total + shift) * v
        for k in range(1, cols):
            acc = acc + base[k] * vc[around[k]]
        norm = jnp.sum(v * v, axis=1, keepdims=True)
        product = jnp.sum(acc, axis=1, keepdims=True)
        line = jnp.where(lane == sub, norm, 0.0) + jnp.where(lane == sub + members, product, 0.0)
        sc[me] = jnp.sum(line, axis=0, keepdims=True)
        to_all(lambda other, where: push(
            sc.at[me], sc.at[me], s_s.at[turn], s_r.at[turn], where))
        await_all(pi, p_r.at[turn])
        image = shift + jnp.sum(pin[turn], axis=0)
        await_all(sc, s_r.at[turn])
        sums = jnp.sum(sc[...], axis=0)
        norm = jnp.sum(jnp.where(lane == sub, sums, 0.0), axis=1, keepdims=True)
        product = jnp.sum(jnp.where(lane == sub + members, sums, 0.0), axis=1, keepdims=True)
        return image, norm, product

    image, norm, product = operate(0, rhs)
    alpha = norm / product
    residual = rhs - alpha * image
    image_next, norm_next, product = operate(1, residual)
    ratio = norm_next / norm
    alpha_next = norm_next / (product - ratio * norm_next / alpha)
    out[0] = alpha * rhs + alpha_next * (residual + ratio * rhs)
    out[1] = residual - alpha_next * (image_next + ratio * image)

    await_all(zrow, zr_s)
    await_all(zcol, zc_s)
    await_all(tsend, t_s)
    await_all(isend, i_s)
    for turn in range(2):
        await_all(vrow.at[turn], vr_s.at[turn])
        await_all(vcol.at[turn], vc_s.at[turn])
        await_all(pout.at[turn], p_s.at[turn])
        await_all(scal.at[turn], s_s.at[turn])


def local(rows, cols, covariates, lengthscale, nugget, patch_values, patch_weights, block_index,
          slot_count, owner):
    devices = rows * cols
    feats, st = covariates.shape
    held, members, cells = patch_values.shape
    slots = patch_weights.shape[1]
    cap = max(128 // slots, 2 * held // devices)
    wide = -(-(6 * feats + 8) // 128) * 128
    dma = pltpu.SemaphoreType.DMA
    vmem = pltpu.VMEM
    scratch = [
        vmem((held * members, cells), patch_values.dtype),
        vmem((held * slots, cells), patch_weights.dtype),
        vmem((rows, feats, st), F32),
        vmem((cols, feats, st), F32),
        vmem((rows * st, wide), BF16),
        vmem((cols, wide, st), BF16),
        vmem((cols, rows * st, st), BF16),
        vmem((cols, rows * st, st), BF16),
        vmem((devices, cap, slots * members), F32),
        vmem((devices, cap, slots * members), F32),
        vmem((devices, 1, 128), F32),
        vmem((devices, 1, 128), F32),
        vmem((2, rows, members, st), F32),
        vmem((2, cols, members, st), F32),
        vmem((cols, members, st), F32),
        vmem((2, cols, members, st), F32),
        vmem((2, cols, members, st), F32),
        vmem((2, devices, 1, 128), F32),
    ]
    scratch += [dma((2,))] + [dma(())] * 8 + [dma((2,))] * 8
    spec = pl.BlockSpec(memory_space=pltpu.VMEM)
    far = pl.BlockSpec(memory_space=pl.ANY)
    both = pl.pallas_call(
        functools.partial(kernel, rows, cols, cap),
        out_shape=jax.ShapeDtypeStruct((2, members, st), F32),
        in_specs=[spec, spec, spec, far, far, spec, spec, spec],
        out_specs=spec,
        scratch_shapes=scratch,
        compiler_params=pltpu.CompilerParams(
            collective_id=0, has_side_effects=True, vmem_limit_bytes=56 * 2**20),
    )(
        covariates,
        lengthscale.reshape(1, feats),
        nugget.reshape(1, st),
        patch_values.reshape(held * members, cells),
        patch_weights.reshape(held * slots, cells),
        block_index.T,
        slot_count.reshape(1, held),
        owner.reshape(1, held),
    )
    return both[0], both[1]


def solution(mesh):
    placed = (
        P(None, ("row", "col")),
        P(),
        P(("row", "col")),
        P(("row", "col"), None, None),
        P(("row", "col"), None, None),
        P(("row", "col"), None),
        P(("row", "col")),
        P(("row", "col"), None),
    )
    return jax.shard_map(
        functools.partial(local, mesh.shape["row"], mesh.shape["col"]),
        mesh=mesh,
        in_specs=placed,
        out_specs=(P(None, ("row", "col")), P(None, ("row", "col"))),
        check_vma=False,
    )
```

time: 61.9 us -> 43.1 us (0.70)
  Pallas kernels: 56.8 us -> 40.9 us
  local copies, waits for them, and re-layouts: 4.19 us -> 1.35 us
    pallas_call x1, Pallas kernels: 56.8 us -> 40.9 us  [local(): pl.pallas_call(functools.partial(kernel, rows, cols, cap), out_shape=jax....]
    unnamed x10 -> x0, local copies, waits for them, and re-layouts: 4.19 us -> none
    squeeze x0 -> x1, local copies, waits for them, and re-layouts: none -> 1.35 us  [local(): return (both[0], both[1])]
where the time goes in v2:
time: 43.1 us; the launch traced here: 42.9 us
  Pallas kernels  40.9 us (95%)
  local copies, waits for them, and re-layouts  1.35 us (3%)
  between operations  0.64 us (1%)
    pallas_call x1, Pallas kernels, local(): pl.pallas_call(functools.partial(kernel, rows, cols, cap), out_shape=jax....  40.9 us
    squeeze x1, local copies, waits for them, and re-layouts, local(): return (both[0], both[1])  1.35 us

profile of v2, /device:TPU:0, one launch (start us, length us, event | category | flops | bytes accessed | tf_op | source)
XLA Modules:
  0.0 42.9 jit_solution(17088982564204015653)
XLA Ops:
  0.6 40.9 %shard_map.95 = f32[2,16,256]{2,1,0:T(8,128)} custom-call(f32[16,256]{1,0:T(8,128)} %cov.1, f32[1,16]{1,0:T(1,128)} %bitcast.17, f32[1,256]{1,0:T(1,128)} %bitcast.14, bf16[4096,128]{1,0:T(8,128)(2,1)} %bitcast.11, bf16[2048,128]{1,0:T(8,128)(2,1)} %bitcast.12, s32[8,256]{1,0:T(8,128)} %bitcast.13, s32[1,256]{1,0:T(1,128)} %bitcast.15, s32[1,256]{1,0:T(1,128)} %bitcast.16), custom_call_target="tpu_custom_call" | custom-call | tf_op jit(solution)/shard_map/pallas_call | solution.py:340
  41.5 1.3 %slice_bitcast_fusion = (f32[16,256]{1,0:T(8,128)}, f32[16,256]{1,0:T(8,128)}) fusion(f32[2,16,256]{2,1,0:T(8,128)} %shard_map.95), kind=kLoop, calls=%fused_computation | loop fusion | bytes 65536 | tf_op jit(solution)/shard_map/squeeze | solution.py:358

commit v3 on v2

--- a/solution.py
+++ b/solution.py
@@ -70,7 +70,7 @@
     cov, ls, nug, val_hbm, wts_hbm, idx, cnt, own,
     out,
     val, wts, zrow, zcol, left, right, k_hi, k_lo,
-    tsend, trecv, isend, irecv, vrow, vcol, base, pout, pin, scal,
+    tsend, trecv, isend, irecv, vrow, vcol, pout, pin, scal,
     load, zr_s, zr_r, zc_s, zc_r, t_s, t_r, i_s, i_r,
     vr_s, vr_r, vc_s, vc_r, p_s, p_r, s_s, s_r,
 ):
@@ -191,19 +191,15 @@
 
     to_all(send_terms)
 
+    await_all(zcol, zc_r)
+    for k in range(cols):
+        left[k * st : (k + 1) * st, :] = features(zcol[around[k]], True).T.astype(BF16)
     await_all(zrow, zr_r)
     for k in range(rows):
-        left[k * st : (k + 1) * st, :] = features(zrow[row_of(k)], True).T.astype(BF16)
-    await_all(zcol, zc_r)
-
-    def make_right(k, carry):
-        right[k] = features(zcol[col_of(k)], False).astype(BF16)
-        return carry
-
-    lax.fori_loop(0, cols, make_right, 0)
+        right[k] = features(zrow[row_of(k)], False).astype(BF16)
 
     chunk = 2 * st
-    chunks = rows * st // chunk
+    chunks = cols * st // chunk
 
     def make_kernel(j, carry):
         for i in range(chunks):
@@ -216,7 +212,7 @@
             k_lo[j, here, :] = low
         return carry
 
-    lax.fori_loop(0, cols, make_kernel, 0)
+    lax.fori_loop(0, rows, make_kernel, 0)
 
     await_all(irecv, i_r)
     got = devices * cap
@@ -242,34 +238,35 @@
         po, pi = pout.at[turn], pin.at[turn]
         vr[r] = v
         vc[c] = v
+        for k in range(1, cols):
+            push(vc.at[c], vc.at[c], vc_s.at[turn], vc_r.at[turn, cols - k], (r, around[k]))
         to_row(lambda other, where: push(
             vr.at[r], vr.at[r], vr_s.at[turn], vr_r.at[turn], where))
-        to_col(lambda other, where: push(
-            vc.at[c], vc.at[c], vc_s.at[turn], vc_r.at[turn], where))
-
-        def part(parts, k, here):
-            hi, low = parts
-            double = mm(jnp.concatenate([hi, low], axis=0), k_hi[k, here, :])
-            return double[:members] + double[members:] + mm(hi, k_lo[k, here, :])
-
-        mine = split2(v)
-        for k in range(cols):
-            base[k] = part(mine, k, pl.ds(0, st))
+
+        total = [jnp.zeros((members, st), F32)] * rows
+        order = sorted(range(cols), key=lambda k: min(k, cols - k))
+        for k in order:
+            if k:
+                part = vc.at[around[k]]
+                pltpu.make_async_copy(part, part, vc_r.at[turn, k]).wait()
+            block = vc[around[k]] if k else v
+            hi, low = split2(block)
+            both = jnp.concatenate([hi, low], axis=0)
+            here = pl.ds(k * st, st)
+            for j in range(rows):
+                double = mm(both, k_hi[j, here, :])
+                single = mm(hi, k_lo[j, here, :])
+                total[j] = total[j] + (double[:members] + (double[members:] + single))
+        for j in range(1, rows):
+            other = row_of(j)
+            po[other] = total[j]
+            push(po.at[other], pi.at[r], p_s.at[turn], p_r.at[turn], (other, c))
+        pi[r] = total[0]
+        shift = nug[...] * v
         await_all(vr, vr_r.at[turn])
-        others = split2(jnp.concatenate([vr[row_of(k)] for k in range(1, rows)], axis=1))
-        rest = pl.ds(st, (rows - 1) * st)
-        for k in range(1, cols):
-            total = base[k] + part(others, k, rest)
-            base[k] = total
-            po[around[k]] = total
-            push(po.at[around[k]], pi.at[c], p_s.at[turn], p_r.at[turn], (r, around[k]))
-        total = base[0] + part(others, 0, rest)
-        pi[c] = total
-        shift = nug[...] * v
-        await_all(vc, vc_r.at[turn])
-        acc = (total + shift) * v
-        for k in range(1, cols):
-            acc = acc + base[k] * vc[around[k]]
+        acc = (total[0] + shift) * v
+        for j in range(1, rows):
+            acc = acc + total[j] * vr[row_of(j)]
         norm = jnp.sum(v * v, axis=1, keepdims=True)
         product = jnp.sum(acc, axis=1, keepdims=True)
         line = jnp.where(lane == sub, norm, 0.0) + jnp.where(lane == sub + members, product, 0.0)
@@ -319,22 +316,21 @@
         vmem((held * slots, cells), patch_weights.dtype),
         vmem((rows, feats, st), F32),
         vmem((cols, feats, st), F32),
-        vmem((rows * st, wide), BF16),
-        vmem((cols, wide, st), BF16),
-        vmem((cols, rows * st, st), BF16),
-        vmem((cols, rows * st, st), BF16),
+        vmem((cols * st, wide), BF16),
+        vmem((rows, wide, st), BF16),
+        vmem((rows, cols * st, st), BF16),
+        vmem((rows, cols * st, st), BF16),
         vmem((devices, cap, slots * members), F32),
         vmem((devices, cap, slots * members), F32),
         vmem((devices, 1, 128), F32),
         vmem((devices, 1, 128), F32),
         vmem((2, rows, members, st), F32),
         vmem((2, cols, members, st), F32),
-        vmem((cols, members, st), F32),
-        vmem((2, cols, members, st), F32),
-        vmem((2, cols, members, st), F32),
+        vmem((2, rows, members, st), F32),
+        vmem((2, rows, members, st), F32),
         vmem((2, devices, 1, 128), F32),
     ]
-    scratch += [dma((2,))] + [dma(())] * 8 + [dma((2,))] * 8
+    scratch += [dma((2,))] + [dma(())] * 8 + [dma((2,))] * 3 + [dma((2, cols))] + [dma((2,))] * 4
     spec = pl.BlockSpec(memory_space=pltpu.VMEM)
     far = pl.BlockSpec(memory_space=pl.ANY)
     both = pl.pallas_call(

time: 43.1 us -> 45.8 us (1.063)
  Pallas kernels: 40.9 us -> 43.6 us
    pallas_call x1, Pallas kernels: 40.9 us -> 43.6 us  [local(): pl.pallas_call(functools.partial(kernel, rows, cols, cap), out_shape=jax....]
where the time goes in v3:
time: 45.8 us; the launch traced here: 45.5 us
  Pallas kernels  43.6 us (95%)
  local copies, waits for them, and re-layouts  1.35 us (3%)
  between operations  0.64 us (1%)
    pallas_call x1, Pallas kernels, local(): pl.pallas_call(functools.partial(kernel, rows, cols, cap), out_shape=jax....  43.6 us
    squeeze x1, local copies, waits for them, and re-layouts, local(): return (both[0], both[1])  1.35 us

profile of v3, /device:TPU:0, one launch (start us, length us, event | category | flops | bytes accessed | tf_op | source)
XLA Modules:
  0.0 45.5 jit_solution(16467702653132910867)
XLA Ops:
  0.6 43.6 %shard_map.95 = f32[2,16,256]{2,1,0:T(8,128)} custom-call(f32[16,256]{1,0:T(8,128)} %cov.1, f32[1,16]{1,0:T(1,128)} %bitcast.17, f32[1,256]{1,0:T(1,128)} %bitcast.14, bf16[4096,128]{1,0:T(8,128)(2,1)} %bitcast.11, bf16[2048,128]{1,0:T(8,128)(2,1)} %bitcast.12, s32[8,256]{1,0:T(8,128)} %bitcast.13, s32[1,256]{1,0:T(1,128)} %bitcast.15, s32[1,256]{1,0:T(1,128)} %bitcast.16), custom_call_target="tpu_custom_call" | custom-call | tf_op jit(solution)/shard_map/pallas_call | solution.py:336
  44.2 1.3 %slice_bitcast_fusion = (f32[16,256]{1,0:T(8,128)}, f32[16,256]{1,0:T(8,128)}) fusion(f32[2,16,256]{2,1,0:T(8,128)} %shard_map.95), kind=kLoop, calls=%fused_computation | loop fusion | bytes 65536 | tf_op jit(solution)/shard_map/squeeze | solution.py:354

commit v4 on v2

--- a/solution.py
+++ b/solution.py
@@ -162,7 +162,6 @@
     blocks = iota((group, members, 128), 0) == iota((group, members, 128), 2) // slots
     lane_patch = iota((group, 128), 1) // slots == iota((group, 128), 0)
     slot_of = iota((members, 128), 1) % slots
-    total = jnp.zeros((devices * cap, 2 * slots * members), F32)
     tables, spreads = [], []
     for g in range(held // group):
         cross = mm_nt(
@@ -178,9 +177,7 @@
             jnp.where(lane_patch, position[g * group : (g + 1) * group], 0.0), axis=0, keepdims=True)
         tables.append(
             jnp.where(iota((devices * cap, 128), 0).astype(F32) == at, 1.0, 0.0).astype(BF16))
-        if len(tables) == 4 or g + 1 == held // group:
-            total = total + mm_nt(jnp.concatenate(tables, axis=1), jnp.concatenate(spreads, axis=1))
-            tables, spreads = [], []
+    total = mm_nt(jnp.concatenate(tables, axis=1), jnp.concatenate(spreads, axis=1))
     packed = total[:, : slots * members] + total[:, slots * members :]
     tsend[...] = packed.reshape(devices, cap, slots * members)
     trecv[me] = tsend[me]
@@ -196,18 +193,15 @@
         left[k * st : (k + 1) * st, :] = features(zrow[row_of(k)], True).T.astype(BF16)
     await_all(zcol, zc_r)
 
-    def make_right(k, carry):
-        right[k] = features(zcol[col_of(k)], False).astype(BF16)
-        return carry
-
-    lax.fori_loop(0, cols, make_right, 0)
+    for k in range(cols):
+        right[k] = features(zcol[around[k]], False).astype(BF16)
 
     chunk = 2 * st
     chunks = rows * st // chunk
 
-    def make_kernel(j, carry):
-        for i in range(chunks):
-            here = pl.ds(i * chunk, chunk)
+    def make_kernel(pair, carry):
+        for t in range(2 * chunks):
+            j, here = 2 * pair + t // chunks, pl.ds(t % chunks * chunk, chunk)
             square = jnp.maximum(mm(left[here, :], right[j]), 1e-30)
             w = square * lax.rsqrt(square)
             value = (1.0 + LINEAR * w + SQUARE * square) * jnp.exp2(-w)
@@ -216,7 +210,7 @@
             k_lo[j, here, :] = low
         return carry
 
-    lax.fori_loop(0, cols, make_kernel, 0)
+    lax.fori_loop(0, cols // 2, make_kernel, 0)
 
     await_all(irecv, i_r)
     got = devices * cap
@@ -258,7 +252,7 @@
         await_all(vr, vr_r.at[turn])
         others = split2(jnp.concatenate([vr[row_of(k)] for k in range(1, rows)], axis=1))
         rest = pl.ds(st, (rows - 1) * st)
-        for k in range(1, cols):
+        for k in sorted(range(1, cols), key=lambda k: -min(k, cols - k)):
             total = base[k] + part(others, k, rest)
             base[k] = total
             po[around[k]] = total

time: 43.1 us -> 43.2 us (level)
  no operation moved by 1% of the time
where the time goes in v4:
time: 43.2 us; the launch traced here: 42.9 us
  Pallas kernels  40.9 us (95%)
  local copies, waits for them, and re-layouts  1.35 us (3%)
  between operations  0.64 us (1%)
    pallas_call x1, Pallas kernels, local(): pl.pallas_call(functools.partial(kernel, rows, cols, cap), out_shape=jax....  40.9 us
    squeeze x1, local copies, waits for them, and re-layouts, local(): return (both[0], both[1])  1.35 us

profile of v4, /device:TPU:0, one launch (start us, length us, event | category | flops | bytes accessed | tf_op | source)
XLA Modules:
  0.0 42.9 jit_solution(8864202747591304614)
XLA Ops:
  0.6 40.9 %shard_map.95 = f32[2,16,256]{2,1,0:T(8,128)} custom-call(f32[16,256]{1,0:T(8,128)} %cov.1, f32[1,16]{1,0:T(1,128)} %bitcast.17, f32[1,256]{1,0:T(1,128)} %bitcast.14, bf16[4096,128]{1,0:T(8,128)(2,1)} %bitcast.11, bf16[2048,128]{1,0:T(8,128)(2,1)} %bitcast.12, s32[8,256]{1,0:T(8,128)} %bitcast.13, s32[1,256]{1,0:T(1,128)} %bitcast.15, s32[1,256]{1,0:T(1,128)} %bitcast.16), custom_call_target="tpu_custom_call" | custom-call | tf_op jit(solution)/shard_map/pallas_call | solution.py:334
  41.6 1.3 %slice_bitcast_fusion = (f32[16,256]{1,0:T(8,128)}, f32[16,256]{1,0:T(8,128)}) fusion(f32[2,16,256]{2,1,0:T(8,128)} %shard_map.95), kind=kLoop, calls=%fused_computation | loop fusion | bytes 65536 | tf_op jit(solution)/shard_map/squeeze | solution.py:352

commit v5 on v2

--- a/solution.py
+++ b/solution.py
@@ -156,6 +156,8 @@
     pl.semaphore_wait(barrier, devices - 1)
     to_row(lambda other, where: push(zrow.at[r], zrow.at[r], zr_s, zr_r, where))
     to_col(lambda other, where: push(zcol.at[c], zcol.at[c], zc_s, zc_r, where))
+
+    to_all(lambda other, where: push(isend.at[other], irecv.at[me], i_s, i_r, where))
 
     for copy in loads:
         copy.wait()
@@ -187,7 +189,6 @@
 
     def send_terms(other, where):
         push(tsend.at[other], trecv.at[me], t_s, t_r, where)
-        push(isend.at[other], irecv.at[me], i_s, i_r, where)
 
     to_all(send_terms)
 

time: 43.1 us -> 43 us (level)
  no operation moved by 1% of the time
where the time goes in v5:
time: 43 us; the launch traced here: 42.7 us
  Pallas kernels  40.7 us (95%)
  local copies, waits for them, and re-layouts  1.35 us (3%)
  between operations  0.64 us (1%)
    pallas_call x1, Pallas kernels, local(): pl.pallas_call(functools.partial(kernel, rows, cols, cap), out_shape=jax....  40.7 us
    squeeze x1, local copies, waits for them, and re-layouts, local(): return (both[0], both[1])  1.35 us

profile of v5, /device:TPU:0, one launch (start us, length us, event | category | flops | bytes accessed | tf_op | source)
XLA Modules:
  0.0 42.7 jit_solution(2761185103443435169)
XLA Ops:
  0.6 40.7 %shard_map.95 = f32[2,16,256]{2,1,0:T(8,128)} custom-call(f32[16,256]{1,0:T(8,128)} %cov.1, f32[1,16]{1,0:T(1,128)} %bitcast.17, f32[1,256]{1,0:T(1,128)} %bitcast.14, bf16[4096,128]{1,0:T(8,128)(2,1)} %bitcast.11, bf16[2048,128]{1,0:T(8,128)(2,1)} %bitcast.12, s32[8,256]{1,0:T(8,128)} %bitcast.13, s32[1,256]{1,0:T(1,128)} %bitcast.15, s32[1,256]{1,0:T(1,128)} %bitcast.16), custom_call_target="tpu_custom_call" | custom-call | tf_op jit(solution)/shard_map/pallas_call | solution.py:341
  41.4 1.3 %slice_bitcast_fusion = (f32[16,256]{1,0:T(8,128)}, f32[16,256]{1,0:T(8,128)}) fusion(f32[2,16,256]{2,1,0:T(8,128)} %shard_map.95), kind=kLoop, calls=%fused_computation | loop fusion | bytes 65536 | tf_op jit(solution)/shard_map/squeeze | solution.py:359
